TPU v7x, 128 devices: a whole 4x4x4 slice. The times are simulated.
128 devices in a mesh: row: 8 (over x_lo, z), col: 16 (over x_hi, y, core).
Axes of the slice: x: 4 (x_hi: 2, x_lo: 2; x = x_hi * 2 + x_lo), y: 4, z: 4, core: 2. Of those that a mesh axis runs over, the one named last changes fastest.
Arguments:
- inverse_block: float32 [12288, 12288], P('row', 'col'), may hold values from -0.14433757 to 0.14433757, as said below
- grid_position: int32 [12288], replicated, may hold values from 0 to 12287, each once
- panel_a: float32 [512, 12288], P('row', 'col'), may hold values from -1.5 to 1.5
- pivot_inverse_a: float32 [512, 512], replicated, may hold values from -6 to 6
- chosen_rows: int32 [8192], replicated, may hold values from 0 to 12287, as said below
- top_panel_b: float32 [512, 512], replicated, may hold values from -1.5 to 1.5
- panel_b: float32 [512, 8192], P('row', 'col'), may hold values from -1.5 to 1.5
- pivot_inverse_b: float32 [512, 512], replicated, may hold values from -6 to 6
Outputs:
- inverse_panel_a: float32 [12288, 512], P(('row', 'col'))
- diagonal_a: float32 [512, 512], replicated
- inverse_panel_b: float32 [12288, 512], P(('row', 'col'))
- inverse_top_b: float32 [512, 512], replicated
- diagonal_b: float32 [512, 512], replicated
Inputs may be any that keep to these rules, and one draw needn't show every extreme that they name: `grid_position`: each of 0 to 12287 appears once. `chosen_rows`: 8192 distinct values. `inverse_block`: symmetric: entry (i, j) equals entry (j, i) in grid storage order.
All inputs are finite; a program needn't handle non-finite values.
Results may differ from a plain program's by a relative error of at most 0.00008.
Values sent between devices are 32-bit elements; how exact they have to be, the bound alone decides.
A program may use at most 128 MiB of HBM per device.

v0:
```python
import jax
import jax.numpy as jnp
from jax import lax
from jax.sharding import PartitionSpec as P


def pick_columns(wide, index, limit):
    valid = (index < limit).astype(jnp.float32)
    taken = jnp.take(wide, jnp.minimum(index, limit - 1), axis=1)
    return taken * valid[None, :]


def select_columns(wide, source, start, length, limit):
    index = lax.dynamic_slice_in_dim(source, start, length, 0)
    return pick_columns(wide, index, limit)


def project(block, panel_t):
    return lax.dot_general(
        block,
        panel_t,
        (((1,), (1,)), ((), ())),
        precision=lax.Precision.HIGHEST,
        preferred_element_type=jnp.float32,
    )


def body(
    inverse_block,
    grid_position,
    panel_a,
    pivot_inverse_a,
    chosen_rows,
    top_panel_b,
    panel_b,
    pivot_inverse_b,
):
    exact = lax.Precision.HIGHEST
    rows_here = inverse_block.shape[0]
    cols_here = inverse_block.shape[1]
    order = grid_position.shape[0]
    count = chosen_rows.shape[0]
    row_count = lax.axis_size("row")
    own_rows = rows_here // lax.axis_size("col")
    col_start = lax.axis_index("col") * cols_here
    own_start = lax.axis_index("row") * rows_here + lax.axis_index("col") * own_rows
    group_starts = (
        jnp.arange(row_count, dtype=jnp.int32) * rows_here + lax.axis_index("col") * own_rows
    )
    group_index = (group_starts[:, None] + jnp.arange(own_rows, dtype=jnp.int32)[None, :]).reshape(
        -1
    )
    local_offset = lax.axis_index("row") * own_rows
    source_a = (
        jnp.zeros((order,), jnp.int32).at[grid_position].set(jnp.arange(order, dtype=jnp.int32))
    )
    source_b = (
        jnp.full((order,), count, jnp.int32)
        .at[grid_position[chosen_rows]]
        .set(jnp.arange(count, dtype=jnp.int32))
    )
    group_a = source_a[group_index]
    group_b = source_b[group_index]
    valid_own = (lax.dynamic_slice_in_dim(source_b, own_start, own_rows, 0) < count).astype(
        jnp.float32
    )
    wide_a = lax.all_gather(panel_a, "col", axis=1, tiled=True)
    cols_a, group_own_a = (
        lax.all_gather(
            select_columns(wide_a, source_a, col_start, cols_here, order), "row", axis=0, tiled=True
        ),
        lax.all_gather(pick_columns(wide_a, group_a, order), "row", axis=0, tiled=True),
    )
    product_a = lax.psum_scatter(
        project(inverse_block, cols_a), "col", scatter_dimension=0, tiled=True
    )
    wide_b = lax.all_gather(panel_b, "col", axis=1, tiled=True)
    cols_b, group_own_b = (
        lax.all_gather(
            select_columns(wide_b, source_b, col_start, cols_here, count), "row", axis=0, tiled=True
        ),
        lax.all_gather(pick_columns(wide_b, group_b, count), "row", axis=0, tiled=True),
    )
    product_b = lax.psum_scatter(
        project(inverse_block, cols_b), "col", scatter_dimension=0, tiled=True
    )
    own_a = lax.dynamic_slice_in_dim(group_own_a, local_offset, own_rows, 1)
    own_b = lax.dynamic_slice_in_dim(group_own_b, local_offset, own_rows, 1)
    inverse_panel_a = -product_a
    diag_part = jnp.dot(own_a, inverse_panel_a, precision=exact, preferred_element_type=jnp.float32)
    cross_part = lax.dot_general(
        inverse_panel_a,
        own_b,
        (((0,), (1,)), ((), ())),
        precision=exact,
        preferred_element_type=jnp.float32,
    )
    diag_total, cross = lax.psum((diag_part, cross_part), ("row", "col"))
    diagonal_a = pivot_inverse_a - diag_total
    inverse_top_b = -(
        jnp.dot(diagonal_a, top_panel_b, precision=exact, preferred_element_type=jnp.float32)
        + cross
    )
    bottom = product_b + jnp.dot(
        inverse_panel_a, top_panel_b, precision=exact, preferred_element_type=jnp.float32
    )
    inverse_panel_b = -bottom * valid_own[:, None]
    last_part = jnp.dot(own_b, inverse_panel_b, precision=exact, preferred_element_type=jnp.float32)
    last_total = lax.psum(last_part, ("row", "col"))
    diagonal_b = (
        pivot_inverse_b
        - jnp.dot(top_panel_b.T, inverse_top_b, precision=exact, preferred_element_type=jnp.float32)
        - last_total
    )
    return (inverse_panel_a, diagonal_a, inverse_panel_b, inverse_top_b, diagonal_b)


def solution(mesh):
    in_specs = (P("row", "col"), P(), P("row", "col"), P(), P(), P(), P("row", "col"), P())
    out_specs = (P(("row", "col"), None), P(), P(("row", "col"), None), P(), P())
    return jax.shard_map(body, mesh=mesh, in_specs=in_specs, out_specs=out_specs, check_vma=False)
```

profile of v0, /device:TPU:1, one launch (start us, length us, event | category | flops | bytes accessed | tf_op | source)
XLA Modules:
  0.0 630.5 jit_solution(11764547674448368654)
XLA Ops:
  7.2 0.0 all-gather.7.cloned.1.call-start
  7.2 1.9 copy.40
  9.2 0.0 all-gather.7.cloned.1.call-update
  9.2 0.0 all-gather.13.cloned.1.call-start
  9.2 1.7 copy.43
  11.0 0.0 all-gather.13.cloned.1.call-update
  11.0 0.0 all-gather.9.cloned.1.call-start
  11.1 0.8 compare_select_fusion.1
  11.9 45.4 %scatter_custom_fusion = s32[12288]{0:T(1024)S(1)} fusion(s32[12288]{0:T(1024)S(1)} %compare_select_fusion.1, s32[12288]{0:T(1024)S(1)} %iota.15, s32[]{:T(128)} %constant.4.clone.1), kind=kCustom, calls=%fused_computation.35 | custom fusion | bytes 49156 | tf_op jit(solution)/shard_map/scatter | solution.py:55
  57.3 0.1 compare_and_fusion.3
  57.4 21.3 %all-gather.7.cloned.1.call-done = f32[64,12288]{0,1:T(8,128)} async-done(((f32[64,768]{0,1:T(8,128)}), f32[64,12288]{0,1:T(8,128)}) %all-gather.7.cloned.1.call-update) | async-done | bytes 3145744 | tf_op jit(solution)/shard_map/all_gather | solution.py:67
  78.7 4.3 gather_fusion.3
  83.1 0.1 copy.41
  83.3 0.7 bitcast_multiply_fusion.3
  84.0 0.0 all-gather.9.cloned.1.call-update
  84.0 0.0 all-gather.15.cloned.1.call-start
  84.1 45.5 %gather_fusion.1 = s32[8192]{0:T(1024)S(1)} fusion(s32[12288]{0:T(1024)S(1)} %copy-done.1, s32[8192]{0:T(1024)S(1)} %fusion.11), kind=kCustom, calls=%fused_computation.5 | custom fusion | bytes 98304 | tf_op jit(solution)/shard_map/gather | solution.py:59
  129.7 30.5 %scatter_custom_fusion.1 = s32[12288]{0:T(1024)S(1)} fusion(s32[8192]{0:T(1024)S(1)} %bitcast.35, s32[8192]{0:T(1024)S(1)} %iota.17, s32[]{:T(128)} %constant.36.clone.1), kind=kCustom, calls=%fused_computation.33 | custom fusion | bytes 49156 | tf_op jit(solution)/shard_map/scatter | solution.py:60
  160.1 0.1 compare_and_fusion.1
  160.2 0.0 all-gather.13.cloned.1.call-done
  160.3 3.8 gather_fusion.5
  164.1 0.1 copy.44
  164.2 0.7 bitcast_multiply_fusion.1
  164.9 0.0 reduce-scatter.7.cloned.1.call-start
  165.0 4.1 all-gather.9.cloned.1.call-done
  169.1 11.3 %convolution_bitcast_fusion.1 = f32[1536,512]{0,1:T(8,128)} fusion(f32[512,768]{1,0:T(8,128)} %all-gather.9.cloned.1.call-done, f32[1536,768]{1,0:T(8,128)} %param.12), kind=kOutput, calls=%fused_computation.10 | convolution fusion | flops 7247757312 | bytes 9437184 | tf_op jit(solution)/shard_map/dot_general | solution.py:19
  180.3 3.7 copy.52
  184.0 0.0 all-gather.11.cloned.1.call-start
  184.1 0.1 iota_add_fusion
  184.2 0.1 add.114
  184.3 4.5 gather_fusion
  188.8 4.4 gather_fusion.4
  193.2 0.1 copy.42
  193.3 0.7 bitcast_multiply_fusion.2
  194.0 0.0 all-gather.17.cloned.1.call-start
  194.1 4.5 gather_fusion.2
  198.6 3.8 gather_fusion.6
  202.4 0.1 copy.46
  202.5 0.7 bitcast_multiply_fusion
  203.3 0.2 reduce-scatter.9.cloned.1.call-start
  203.5 7.6 %all-gather.15.cloned.1.call-done = f32[512,768]{1,0:T(8,128)} async-done(((f32[64,768]{1,0:T(8,128)}), f32[512,768]{1,0:T(8,128)}) %all-gather.15.cloned.1.call-update) | async-done | bytes 1572880 | tf_op jit(solution)/shard_map/all_gather | solution.py:79
  211.0 11.3 %convolution_bitcast_fusion = f32[1536,512]{0,1:T(8,128)} fusion(f32[512,768]{1,0:T(8,128)} %all-gather.15.cloned.1.call-done, f32[1536,768]{1,0:T(8,128)} %param.12), kind=kOutput, calls=%fused_computation.9 | convolution fusion | flops 7247757312 | bytes 9437184 | tf_op jit(solution)/shard_map/dot_general | solution.py:19
  222.4 3.5 copy.54
  225.9 0.0 all-reduce.3.cloned.1.call-start
  226.0 0.1 compare_convert_fusion.4
  226.0 68.4 %reduce-scatter.7.cloned.1.call-done = f32[96,512]{1,0:T(8,128)} async-done(((f32[1536,512]{1,0:T(8,128)}), f32[96,512]{1,0:T(8,128)}) %reduce-scatter.7.cloned.1.call-update) | async-done | bytes 196624
  294.4 1.0 copy.53
  295.5 35.6 %all-gather.11.cloned.1.call-done = f32[512,768]{1,0:T(8,128)} async-done(((f32[64,768]{1,0:T(8,128)}), f32[512,768]{1,0:T(8,128)}) %all-gather.11.cloned.1.call-update) | async-done | bytes 1572880 | tf_op jit(solution)/shard_map/all_gather | solution.py:72
  331.1 3.0 fusion.5
  334.1 39.1 %all-gather.17.cloned.1.call-done = f32[512,768]{1,0:T(8,128)} async-done(((f32[64,768]{1,0:T(8,128)}), f32[512,768]{1,0:T(8,128)}) %all-gather.17.cloned.1.call-update) | async-done | bytes 1572880 | tf_op jit(solution)/shard_map/all_gather | solution.py:82
  373.2 3.1 fusion.9
  376.3 80.5 %reduce-scatter.9.cloned.1.call-done = f32[96,512]{1,0:T(8,128)} async-done(((f32[1536,512]{1,0:T(8,128)}), f32[96,512]{1,0:T(8,128)}) %reduce-scatter.9.cloned.1.call-update) | async-done | bytes 196624 | tf_op jit(solution)/shard_map/reduce_scatter | solution.py:84
  456.8 1.7 fusion.4
  458.5 0.7 copy-done.7
  459.2 3.1 fusion.7
  462.3 1.6 copy.47
  464.0 0.7 neg.9
  464.7 1.8 copy.49
  466.5 149.7 %all-reduce.3.cloned.1.call-done = (f32[512,512]{1,0:T(8,128)}, f32[512,512]{1,0:T(8,128)}, f32[512,512]{0,1:T(8,128)}) async-done(((f32[512,512]{1,0:T(8,128)}, f32[512,512]{1,0:T(8,128)}, f32[512,512]{0,1:T(8,128)}), (f32[512,512]{1,0:T(8,128)}, f32[512,512]{1,0:T(8,128)}, f32[512,512]{0,1:T(8,128)})) %all-reduce.3.cloned.1.call-update) | async-done | bytes 3145744 | tf_op jit(solution)/shard_map/psum | solution.py:98
  616.2 1.6 sub.9
  617.8 1.9 fusion.2
  619.7 1.0 copy-done.3
  620.6 2.0 fusion.1
  622.6 1.3 copy.50
  (37 shorter events, 0.3 us)
Async XLA Ops:
  7.2 449.7 %copy-start = (f32[512,512]{1,0:T(8,128)S(1)}, f32[512,512]{1,0:T(8,128)}, u32[]{:S(2)}) copy-start(f32[512,512]{1,0:T(8,128)} %param.17) | copy-start | bytes 3145732
  7.2 76.9 %copy-start.1 = (s32[12288]{0:T(1024)S(1)}, s32[12288]{0:T(1024)}, u32[]{:S(2)}) copy-start(s32[12288]{0:T(1024)} %param.13) | copy-start | bytes 147460
  7.2 76.8 %copy-start.8 = (s32[8192]{0:T(1024)S(1)}, s32[8192]{0:T(1024)}, u32[]{:S(2)}) copy-start(s32[8192]{0:T(1024)} %param.16) | copy-start | bytes 98308
  7.2 71.5 %all-gather.7.cloned.1.call-start = ((), (), s32[]{:S(2)}) async-start(), calls=%async_computation.2 | async-start | bytes 6684672 | tf_op jit(solution)/shard_map/all_gather | solution.py:67
  9.2 151.1 %all-gather.13.cloned.1.call-start = ((), (), s32[]{:S(2)}) async-start(), calls=%async_computation.5 | async-start | bytes 4456448 | tf_op jit(solution)/shard_map/all_gather | solution.py:77
  11.0 158.0 %all-gather.9.cloned.1.call-start = ((), (), s32[]{:S(2)}) async-start(), calls=%async_computation.3 | async-start | bytes 1769472 | tf_op jit(solution)/shard_map/all_gather | solution.py:69
  84.0 127.1 %all-gather.15.cloned.1.call-start = ((), (), s32[]{:S(2)}) async-start(), calls=%async_computation.6 | async-start | bytes 1769472 | tf_op jit(solution)/shard_map/all_gather | solution.py:79
  164.9 129.5 %reduce-scatter.7.cloned.1.call-start = ((), (), s32[]{:S(2)}) async-start(), calls=%async_computation.8 | async-start | bytes 3342336
  184.0 147.1 %all-gather.11.cloned.1.call-start = ((), (), s32[]{:S(2)}) async-start(), calls=%async_computation.4 | async-start | bytes 1769472 | tf_op jit(solution)/shard_map/all_gather | solution.py:72
  194.0 179.2 %all-gather.17.cloned.1.call-start = ((), (), s32[]{:S(2)}) async-start(), calls=%async_computation.7 | async-start | bytes 1769472 | tf_op jit(solution)/shard_map/all_gather | solution.py:82
  203.3 253.6 %reduce-scatter.9.cloned.1.call-start = ((), (), s32[]{:S(2)}) async-start(), calls=%async_computation.9 | async-start | bytes 3342336 | tf_op jit(solution)/shard_map/reduce_scatter | solution.py:84
  225.9 390.3 %all-reduce.3.cloned.1.call-start = ((), (), s32[]{:S(2)}) async-start(), calls=%async_computation.10 | async-start | bytes 6291456 | tf_op jit(solution)/shard_map/psum | solution.py:98
  458.5 0.7 copy-start.7
  462.3 153.9 %copy-start.4 = (f32[512,512]{1,0:T(8,128)S(1)}, f32[512,512]{1,0:T(8,128)}, u32[]{:S(2)}) copy-start(f32[512,512]{1,0:T(8,128)} %param.15) | copy-start | bytes 3145732
  616.2 1.6 copy-start.6
  616.2 4.5 copy-start.5
  617.7 1.9 copy-start.2
  619.6 1.0 copy-start.3
Sparse Core Ops, SparseCore 0:
  11.1 67.6 all-gather.6
  81.8 53.0 all-gather.12
  137.1 31.9 all-gather.8
  171.1 39.8 all-gather.14
  214.9 79.4 reduce-scatter.6
  296.5 34.5 all-gather.10
  333.3 39.8 all-gather.16
  377.3 79.5 reduce-scatter.8
  462.5 153.5 all-reduce.2
where the time goes:
time: 631 us; the launch traced here: 630 us
  waiting for transfers between devices  406 us (64%)
  local copies, waits for them, and re-layouts  166 us (26%)
  matrix products  37.4 us (6%)
  between operations  14.2 us (2%)
  other arithmetic  6.35 us (1%)
    psum x1, waiting for transfers between devices, body(): diag_total, cross = lax.psum((diag_part, cross_part), ('row', 'col'))  150 us
    reduce_scatter x1, waiting for transfers between devices, body(): lax.psum_scatter(project(inverse_block, cols_b), 'col', scatter_dimension...  80.5 us
    unnamed x10, waiting for transfers between devices  68.6 us
    gather x1, local copies, waits for them, and re-layouts, body(): grid_position[chosen_rows]  45.5 us
    scatter x1, local copies, waits for them, and re-layouts, body(): jnp.zeros((order,), jnp.int32).at[grid_position]  45.4 us
    all_gather x1, waiting for transfers between devices, body(): lax.all_gather(pick_columns(wide_b, group_b, count), 'row', axis=0, tiled...  39.1 us
    all_gather x1, waiting for transfers between devices, body(): lax.all_gather(pick_columns(wide_a, group_a, order), 'row', axis=0, tiled...  35.6 us
    scatter x1, local copies, waits for them, and re-layouts, body(): source_b = jnp.full((order,), count, jnp.int32).at[grid_position[chosen_r...  30.5 us
  transfers between devices with their start and end apart: 9, of which 8 were waited for; matrix products, arithmetic and copies ran while one was open for 31% of the time, Pallas kernels for 0%

commit v1 on v0

--- a/solution.py
+++ b/solution.py
@@ -65,11 +65,20 @@
         jnp.float32
     )
     wide_a = lax.all_gather(panel_a, "col", axis=1, tiled=True)
+
+    def draft_the_floor(original):
+        return jnp.concatenate(
+            lax.all_to_all(
+                jnp.stack([original for _ in range(lax.axis_size("row"))], 0), "row", 0, 0
+            ),
+            0,
+        )
+
     cols_a, group_own_a = (
         lax.all_gather(
             select_columns(wide_a, source_a, col_start, cols_here, order), "row", axis=0, tiled=True
         ),
-        lax.all_gather(pick_columns(wide_a, group_a, order), "row", axis=0, tiled=True),
+        draft_the_floor(pick_columns(wide_a, group_a, order)),
     )
     product_a = lax.psum_scatter(
         project(inverse_block, cols_a), "col", scatter_dimension=0, tiled=True

time: 631 us -> 594 us (0.941)
  waiting for transfers between devices: 406 us -> 364 us
    all_gather x1 -> x0, waiting for transfers between devices: 35.6 us -> none  [body(): lax.all_gather(pick_columns(wide_a, group_a, order), 'row', axis=0, tiled...]
    unnamed x10 -> x9, waiting for transfers between devices: 68.6 us -> 57.5 us
    all_gather x1, waiting for transfers between devices: 7.55 us -> 17.4 us  [body(): lax.all_gather(select_columns(wide_b, source_b, col_start, cols_here, cou...]
  transfers between devices with their start and end apart: 9 -> 9, of which waited for: 8 -> 7; matrix products, arithmetic and copies ran while one was open for 31% -> 33% of each run, Pallas kernels for 0% -> 0%
where the time goes in v1:
time: 594 us; the launch traced here: 593 us
  waiting for transfers between devices  364 us (61%)
  local copies, waits for them, and re-layouts  167 us (28%)
  matrix products  36.4 us (6%)
  between operations  14.5 us (2%)
    psum x1, waiting for transfers between devices, body(): diag_total, cross = lax.psum((diag_part, cross_part), ('row', 'col'))  150 us
    reduce_scatter x1, waiting for transfers between devices, body(): lax.psum_scatter(project(inverse_block, cols_b), 'col', scatter_dimension...  80.5 us
    unnamed x9, waiting for transfers between devices  57.5 us
    gather x1, local copies, waits for them, and re-layouts, body(): grid_position[chosen_rows]  45.5 us
    scatter x1, local copies, waits for them, and re-layouts, body(): jnp.zeros((order,), jnp.int32).at[grid_position]  45.4 us
    all_gather x1, waiting for transfers between devices, body(): lax.all_gather(pick_columns(wide_b, group_b, count), 'row', axis=0, tiled...  33.5 us
    scatter x1, local copies, waits for them, and re-layouts, body(): source_b = jnp.full((order,), count, jnp.int32).at[grid_position[chosen_r...  30.5 us
    dot_general x2, matrix products, project(): lax.dot_general(block, panel_t, (((1,), (1,)), ((), ())), precision=lax.P...  22.6 us
  transfers between devices with their start and end apart: 9, of which 7 were waited for; matrix products, arithmetic and copies ran while one was open for 33% of the time, Pallas kernels for 0%

profile of v1, /device:TPU:1, one launch (start us, length us, event | category | flops | bytes accessed | tf_op | source)
XLA Modules:
  0.0 592.9 jit_solution(11556661665047451897)
XLA Ops:
  7.2 0.0 all-gather.6.cloned.1.call-start
  7.2 1.9 copy.42
  9.2 0.0 all-gather.6.cloned.1.call-update
  9.2 0.0 all-gather.10.cloned.1.call-start
  9.2 1.7 copy.45
  11.0 0.0 all-gather.10.cloned.1.call-update
  11.0 0.0 all-gather.8.cloned.1.call-start
  11.1 0.8 compare_select_fusion.1
  11.9 45.4 %scatter_custom_fusion = s32[12288]{0:T(1024)S(1)} fusion(s32[12288]{0:T(1024)S(1)} %compare_select_fusion.1, s32[12288]{0:T(1024)S(1)} %iota.15, s32[]{:T(128)} %constant.4.clone.1), kind=kCustom, calls=%fused_computation.35 | custom fusion | bytes 49156 | tf_op jit(solution)/shard_map/scatter | solution.py:55
  57.3 0.1 compare_and_fusion.3
  57.4 21.3 %all-gather.6.cloned.1.call-done = f32[64,12288]{0,1:T(8,128)} async-done(((f32[64,768]{0,1:T(8,128)}), f32[64,12288]{0,1:T(8,128)}) %all-gather.6.cloned.1.call-update) | async-done | bytes 3145744 | tf_op jit(solution)/shard_map/all_gather | solution.py:67
  78.7 4.3 gather_fusion.3
  83.1 0.1 copy.43
  83.3 0.7 bitcast_multiply_fusion.3
  84.0 0.0 all-gather.8.cloned.1.call-update
  84.0 0.0 all-gather.12.cloned.1.call-start
  84.1 45.5 %gather_fusion.1 = s32[8192]{0:T(1024)S(1)} fusion(s32[12288]{0:T(1024)S(1)} %copy-done.1, s32[8192]{0:T(1024)S(1)} %fusion.11), kind=kCustom, calls=%fused_computation.5 | custom fusion | bytes 98304 | tf_op jit(solution)/shard_map/gather | solution.py:59
  129.7 30.5 %scatter_custom_fusion.1 = s32[12288]{0:T(1024)S(1)} fusion(s32[8192]{0:T(1024)S(1)} %bitcast.37, s32[8192]{0:T(1024)S(1)} %iota.17, s32[]{:T(128)} %constant.36.clone.1), kind=kCustom, calls=%fused_computation.33 | custom fusion | bytes 49156 | tf_op jit(solution)/shard_map/scatter | solution.py:60
  160.1 0.1 compare_and_fusion.1
  160.2 0.0 all-gather.10.cloned.1.call-done
  160.3 3.8 gather_fusion.5
  164.1 0.1 copy.46
  164.2 0.7 bitcast_multiply_fusion.1
  164.9 0.0 all-gather.12.cloned.1.call-update
  164.9 0.0 reduce-scatter.7.cloned.1.call-start
  165.0 4.1 all-gather.8.cloned.1.call-done
  169.1 11.3 %convolution_bitcast_fusion.1 = f32[1536,512]{0,1:T(8,128)} fusion(f32[512,768]{1,0:T(8,128)} %all-gather.8.cloned.1.call-done, f32[1536,768]{1,0:T(8,128)} %param.12), kind=kOutput, calls=%fused_computation.10 | convolution fusion | flops 7247757312 | bytes 9437184 | tf_op jit(solution)/shard_map/dot_general | solution.py:19
  180.4 3.7 copy.54
  184.0 0.0 all-gather.14.cloned.1.call-start
  184.1 0.1 iota_add_fusion
  184.2 0.1 add.114
  184.3 4.5 gather_fusion.2
  188.8 3.8 gather_fusion.6
  192.6 0.1 copy.48
  192.7 0.7 bitcast_multiply_fusion
  193.5 0.2 reduce-scatter.9.cloned.1.call-start
  193.7 17.4 %all-gather.12.cloned.1.call-done = f32[512,768]{1,0:T(8,128)} async-done(((f32[64,768]{1,0:T(8,128)}), f32[512,768]{1,0:T(8,128)}) %all-gather.12.cloned.1.call-update) | async-done | bytes 1572880 | tf_op jit(solution)/shard_map/all_gather | solution.py:88
  211.1 11.3 %convolution_bitcast_fusion = f32[1536,512]{0,1:T(8,128)} fusion(f32[512,768]{1,0:T(8,128)} %all-gather.12.cloned.1.call-done, f32[1536,768]{1,0:T(8,128)} %param.12), kind=kOutput, calls=%fused_computation.9 | convolution fusion | flops 7247757312 | bytes 9437184 | tf_op jit(solution)/shard_map/dot_general | solution.py:19
  222.4 3.6 copy.56
  226.0 4.5 gather_fusion
  230.5 4.6 gather_fusion.4
  235.1 0.1 copy.44
  235.3 1.3 stack.2
  236.6 4.4 all-to-all-start
  241.0 0.3 all-reduce.3.cloned.1.call-start
  241.3 0.1 compare_convert_fusion.4
  241.3 57.4 %reduce-scatter.7.cloned.1.call-done = f32[96,512]{1,0:T(8,128)} async-done(((f32[1536,512]{1,0:T(8,128)}), f32[96,512]{1,0:T(8,128)}) %reduce-scatter.7.cloned.1.call-update) | async-done | bytes 196624
  298.7 1.0 copy.55
  299.8 2.0 fusion.5
  301.8 33.5 %all-gather.14.cloned.1.call-done = f32[512,768]{1,0:T(8,128)} async-done(((f32[64,768]{1,0:T(8,128)}), f32[512,768]{1,0:T(8,128)}) %all-gather.14.cloned.1.call-update) | async-done | bytes 1572880 | tf_op jit(solution)/shard_map/all_gather | solution.py:91
  335.4 3.1 fusion.9
  338.5 80.5 %reduce-scatter.9.cloned.1.call-done = f32[96,512]{1,0:T(8,128)} async-done(((f32[1536,512]{1,0:T(8,128)}), f32[96,512]{1,0:T(8,128)}) %reduce-scatter.9.cloned.1.call-update) | async-done | bytes 196624 | tf_op jit(solution)/shard_map/reduce_scatter | solution.py:93
  419.0 1.7 fusion.4
  420.6 0.7 copy-done.7
  421.3 3.1 fusion.7
  424.5 1.6 copy.49
  426.1 0.7 neg.9
  426.8 1.8 copy.51
  428.6 149.7 %all-reduce.3.cloned.1.call-done = (f32[512,512]{1,0:T(8,128)}, f32[512,512]{1,0:T(8,128)}, f32[512,512]{0,1:T(8,128)}) async-done(((f32[512,512]{1,0:T(8,128)}, f32[512,512]{1,0:T(8,128)}, f32[512,512]{0,1:T(8,128)}), (f32[512,512]{1,0:T(8,128)}, f32[512,512]{1,0:T(8,128)}, f32[512,512]{0,1:T(8,128)})) %all-reduce.3.cloned.1.call-update) | async-done | bytes 3145744 | tf_op jit(solution)/shard_map/psum | solution.py:107
  578.3 1.6 sub.9
  579.9 1.9 fusion.2
  581.8 1.0 copy-done.3
  582.8 2.0 fusion.1
  584.8 1.3 copy.52
  (37 shorter events, 0.3 us)
Async XLA Ops:
  7.2 411.8 %copy-start = (f32[512,512]{1,0:T(8,128)S(1)}, f32[512,512]{1,0:T(8,128)}, u32[]{:S(2)}) copy-start(f32[512,512]{1,0:T(8,128)} %param.17) | copy-start | bytes 3145732
  7.2 76.9 %copy-start.1 = (s32[12288]{0:T(1024)S(1)}, s32[12288]{0:T(1024)}, u32[]{:S(2)}) copy-start(s32[12288]{0:T(1024)} %param.13) | copy-start | bytes 147460
  7.2 76.8 %copy-start.8 = (s32[8192]{0:T(1024)S(1)}, s32[8192]{0:T(1024)}, u32[]{:S(2)}) copy-start(s32[8192]{0:T(1024)} %param.16) | copy-start | bytes 98308
  7.2 71.5 %all-gather.6.cloned.1.call-start = ((), (), s32[]{:S(2)}) async-start(), calls=%async_computation.3 | async-start | bytes 6684672 | tf_op jit(solution)/shard_map/all_gather | solution.py:67
  9.2 151.1 %all-gather.10.cloned.1.call-start = ((), (), s32[]{:S(2)}) async-start(), calls=%async_computation.5 | async-start | bytes 4456448 | tf_op jit(solution)/shard_map/all_gather | solution.py:86
  11.0 158.0 %all-gather.8.cloned.1.call-start = ((), (), s32[]{:S(2)}) async-start(), calls=%async_computation.4 | async-start | bytes 1769472 | tf_op jit(solution)/shard_map/all_gather | solution.py:78
  84.0 127.1 %all-gather.12.cloned.1.call-start = ((), (), s32[]{:S(2)}) async-start(), calls=%async_computation.6 | async-start | bytes 1769472 | tf_op jit(solution)/shard_map/all_gather | solution.py:88
  164.9 133.8 %reduce-scatter.7.cloned.1.call-start = ((), (), s32[]{:S(2)}) async-start(), calls=%async_computation.8 | async-start | bytes 3342336
  184.0 151.3 %all-gather.14.cloned.1.call-start = ((), (), s32[]{:S(2)}) async-start(), calls=%async_computation.7 | async-start | bytes 1769472 | tf_op jit(solution)/shard_map/all_gather | solution.py:91
  193.5 225.5 %reduce-scatter.9.cloned.1.call-start = ((), (), s32[]{:S(2)}) async-start(), calls=%async_computation.9 | async-start | bytes 3342336 | tf_op jit(solution)/shard_map/reduce_scatter | solution.py:93
  236.6 63.2 %all-to-all-start = ((f32[8,64,768]{2,1,0:T(8,128)}), f32[8,64,768]{2,1,0:T(8,128)S(1)}, u32[]{:S(2)}, u32[]{:S(2)}) async-start(f32[8,64,768]{2,1,0:T(8,128)} %stack.2), calls=%async_computation | async-start | bytes 3145728 | tf_op jit(solution)/shard_map/all_to_all | solution.py:71
  241.0 337.3 %all-reduce.3.cloned.1.call-start = ((), (), s32[]{:S(2)}) async-start(), calls=%async_computation.10 | async-start | bytes 6291456 | tf_op jit(solution)/shard_map/psum | solution.py:107
  420.6 0.7 copy-start.7
  424.4 153.9 %copy-start.4 = (f32[512,512]{1,0:T(8,128)S(1)}, f32[512,512]{1,0:T(8,128)}, u32[]{:S(2)}) copy-start(f32[512,512]{1,0:T(8,128)} %param.15) | copy-start | bytes 3145732
  578.3 1.6 copy-start.6
  578.3 4.5 copy-start.5
  579.9 1.9 copy-start.2
  581.8 1.0 copy-start.3
Sparse Core Ops, SparseCore 0:
  11.1 67.6 all-gather.5
  81.8 53.0 all-gather.9
  137.1 31.9 all-gather.7
  171.1 39.8 all-gather.11
  215.0 83.7 reduce-scatter.6
  300.8 34.4 all-gather.13
  339.4 79.5 reduce-scatter.8
  424.6 153.6 all-reduce.2
